TPU v7x, 32 devices: a whole 2x2x4 slice. The times are simulated.
32 devices in a mesh: dp: 8 (over y, x, core), ctx: 4 (over z).
Axes of the slice: x: 2, y: 2, z: 4, core: 2. Of those that a mesh axis runs over, the one named last changes fastest.
Arguments:
- queries: bfloat16 [8, 4, 128, 2048], P('dp', 'ctx'), may hold values from -2.5 to 2.5
- rotated_key_rows: bfloat16 [8, 4, 128, 512], P('dp', 'ctx'), may hold values from -2.5 to 2.5
- values: bfloat16 [8, 4, 128, 512], P('dp', 'ctx'), may hold values from -6 to 6
- cotangent: bfloat16 [8, 4, 128, 2048], P('dp', 'ctx'), may hold values from -6 to 6
- hidden: bfloat16 [8, 4, 128, 4096], P('dp', 'ctx'), may hold values from -6 to 6
- adapter_down_weight: bfloat16 [4096, 16], replicated, may hold values from -0.09375 to 0.09375
- adapter_up_weight: bfloat16 [16, 512], replicated, may hold values from -1.5 to 1.5
- segment_text_length: int32 [8, 4], P('dp', 'ctx'), may hold values from 19 to 78, as said below
Outputs:
- grad_queries: bfloat16 [8, 4, 128, 2048], P('dp', 'ctx')
- grad_keys: bfloat16 [8, 4, 128, 512], P('dp', 'ctx')
- grad_values: bfloat16 [8, 4, 128, 512], P('dp', 'ctx')
- grad_down: float32 [4096, 16], replicated
- grad_up: float32 [16, 512], replicated
Inputs may be any that keep to these rules, and one draw needn't show every extreme that they name: `segment_text_length`: every log has a segment with exactly 78 text tokens and another with the fewest.
All inputs are finite; a program needn't handle non-finite values.
Results may differ from a plain program's by a relative error of at most 0.0019.
The roundings to bfloat16 on the way count: a program that leaves them out, or rounds other values in their place, can miss the bound.
Values may be sent and summed in bfloat16 or wider, within the bound.
A program may use at most 64 MiB of HBM per device.

v0:
```python
import math

import jax
import jax.numpy as jnp
from jax import lax
from jax.sharding import PartitionSpec as P

HEAD_SIZE = 128
SUMM = 50


adapter_scale = 2.0


def group_grads(query_group, key_group, value_group, cot_group, key_mask):
    softmax_scale = 1.0 / math.sqrt(HEAD_SIZE)
    scores = (
        jnp.einsum("tgd,md->gtm", query_group, key_group, preferred_element_type=jnp.float32)
        * softmax_scale
    )
    unnorm = jnp.exp(jnp.where(key_mask[None], scores, -jnp.inf))
    attend = unnorm / jnp.sum(unnorm, -1, keepdims=True)
    attend_grad = jnp.einsum(
        "tgd,md->gtm", cot_group, value_group, preferred_element_type=jnp.float32
    )
    row_dot = jnp.sum(attend * attend_grad, -1, keepdims=True)
    dscore = (attend * (attend_grad - row_dot)).astype(jnp.bfloat16)
    attend_low = attend.astype(jnp.bfloat16)
    query_grad = (
        jnp.einsum("gtm,md->tgd", dscore, key_group, preferred_element_type=jnp.float32)
        * softmax_scale
    )
    key_grad = (
        jnp.einsum("gtm,tgd->md", dscore, query_group, preferred_element_type=jnp.float32)
        * softmax_scale
    )
    value_grad = jnp.einsum(
        "gtm,tgd->md", attend_low, cot_group, preferred_element_type=jnp.float32
    )
    return (query_grad, key_grad, value_grad)


def adapter_terms(hidden_piece, low_rank_piece, value_piece, adapter_up_weight):
    contract = (((0,), (0,)), ((), ()))
    backward_step = lax.dot_general(
        value_piece, adapter_up_weight, (((1,), (1,)), ((), ())), preferred_element_type=jnp.float32
    ).astype(jnp.bfloat16)
    down_part = lax.dot_general(
        hidden_piece, backward_step, contract, preferred_element_type=jnp.float32
    )
    up_part = lax.dot_general(
        low_rank_piece, value_piece, contract, preferred_element_type=jnp.float32
    )
    return (down_part, up_part)


def per_device(
    queries,
    rotated_key_rows,
    values,
    cotangent,
    hidden,
    adapter_down_weight,
    adapter_up_weight,
    segment_text_length,
):
    query_rows = queries[0, 0]
    key_local = rotated_key_rows[0, 0]
    value_local = values[0, 0]
    cot_rows = cotangent[0, 0]
    hidden_row_block = hidden[0, 0]
    length = segment_text_length[0, 0]
    position = lax.axis_index("ctx")
    segment_list = lax.axis_size("ctx")
    log_batch = lax.axis_size("dp")
    tokens = query_rows.shape[0]
    width = key_local.shape[1]
    kv_heads = width // HEAD_SIZE
    groups = query_rows.shape[1] // width
    live = length + SUMM
    rows = jnp.arange(tokens)
    cot_rows = jnp.where((rows < live)[:, None], cot_rows, jnp.zeros_like(cot_rows))
    own_keys = lax.dynamic_slice_in_dim(key_local, length, SUMM, 0)
    own_values = lax.dynamic_slice_in_dim(value_local, length, SUMM, 0)
    memory_keys, memory_values = (
        lax.all_gather(own_keys, "ctx", axis=0, tiled=True),
        lax.all_gather(own_values, "ctx", axis=0, tiled=True),
    )
    count = memory_keys.shape[0]
    memory_owner = jnp.arange(count) // SUMM
    local_mask = (rows[None, :] <= rows[:, None]) & (rows[None, :] < live)
    memory_mask = jnp.broadcast_to((memory_owner < position)[None, :], (tokens, count))
    key_mask = jnp.concatenate([memory_mask, local_mask], axis=1)
    all_keys = jnp.concatenate([memory_keys, key_local], 0)
    all_values = jnp.concatenate([memory_values, value_local], 0)
    query_parts, key_parts, value_parts = ([], [], [])
    for group in range(kv_heads):
        qcols = slice(group * groups * HEAD_SIZE, (group + 1) * groups * HEAD_SIZE)
        kcols = slice(group * HEAD_SIZE, (group + 1) * HEAD_SIZE)
        query_grad, key_grad, value_grad = group_grads(
            query_rows[:, qcols].reshape(tokens, groups, HEAD_SIZE),
            all_keys[:, kcols],
            all_values[:, kcols],
            cot_rows[:, qcols].reshape(tokens, groups, HEAD_SIZE),
            key_mask,
        )
        query_parts.append(query_grad.reshape(tokens, groups * HEAD_SIZE))
        key_parts.append(key_grad)
        value_parts.append(value_grad)
    query_out = jnp.concatenate(query_parts, 1).astype(jnp.bfloat16)
    key_grad = jnp.concatenate(key_parts, 1)
    value_grad = jnp.concatenate(value_parts, 1)
    memory_key_grad, local_key = (key_grad[:count], key_grad[count:])
    memory_value_grad, local_value = (value_grad[:count], value_grad[count:])
    back_key, back_value = (
        lax.psum_scatter(memory_key_grad, "ctx", scatter_dimension=0, tiled=True),
        lax.psum_scatter(memory_value_grad, "ctx", scatter_dimension=0, tiled=True),
    )
    key_out = (
        local_key + lax.dynamic_update_slice_in_dim(jnp.zeros_like(local_key), back_key, length, 0)
    ).astype(jnp.bfloat16)
    value_result = (
        local_value
        + lax.dynamic_update_slice_in_dim(jnp.zeros_like(local_value), back_value, length, 0)
    ).astype(jnp.bfloat16)
    low_rank_rows = jnp.dot(
        hidden_row_block, adapter_down_weight, preferred_element_type=jnp.float32
    ).astype(jnp.bfloat16)
    down_sum, up_sum = lax.psum(
        adapter_terms(hidden_row_block, low_rank_rows, value_result, adapter_up_weight),
        ("dp", "ctx"),
    )
    adapter_factor = adapter_scale / (log_batch * segment_list)
    return (
        query_out[None, None],
        key_out[None, None],
        value_result[None, None],
        down_sum * adapter_factor,
        up_sum * adapter_factor,
    )


def solution(mesh):
    placed = (
        P("dp", "ctx", None, None),
        P("dp", "ctx", None, None),
        P("dp", "ctx", None, None),
        P("dp", "ctx", None, None),
        P("dp", "ctx", None, None),
        P(),
        P(),
        P("dp", "ctx"),
    )
    return jax.shard_map(
        per_device,
        mesh=mesh,
        in_specs=placed,
        out_specs=(
            P("dp", "ctx", None, None),
            P("dp", "ctx", None, None),
            P("dp", "ctx", None, None),
            P(),
            P(),
        ),
        check_vma=False,
    )
```

profile of v0, /device:TPU:25, one launch (start us, length us, event | category | flops | bytes accessed | tf_op | source)
XLA Modules:
  0.0 285.2 jit_solution(11098867364432326245)
XLA Ops:
  8.1 0.9 constant_dynamic-slice_fusion.1
  9.2 11.7 %all-gather.1 = bf16[1,1,200,512]{3,1,0,2:T(2,128)(2,1)S(1)} all-gather(bf16[1,1,50,512]{3,1,0,2:T(2,128)(2,1)S(1)} %copy.106), channel_id=3, replica_groups=mesh['dp'=8,'ctx'=4] {'ctx'}, dimensions={2}, use_global_device_ids=true | all-gather | bytes 256000 | tf_op jit(solution)/shard_map/all_gather | solution.py:87
  21.0 12.8 %all-gather = bf16[1,1,200,512]{3,1,0,2:T(2,128)(2,1)S(1)} all-gather(bf16[1,1,50,512]{3,1,0,2:T(2,128)(2,1)S(1)} %copy.105), channel_id=2, replica_groups=mesh['dp'=8,'ctx'=4] {'ctx'}, dimensions={2}, use_global_device_ids=true | all-gather | bytes 256000 | tf_op jit(solution)/shard_map/all_gather | solution.py:86
  34.1 0.8 fusion.92
  36.6 1.1 convolution_bitcast_fusion.2
  37.7 1.1 convolution_bitcast_fusion.3
  39.0 0.7 fusion.56
  39.9 2.3 multiply_reduce_fusion.2
  42.3 2.1 convolution_bitcast_fusion.7
  44.4 1.2 multiply_convert_fusion.2
  45.6 0.9 fusion.19
  46.5 2.3 multiply_reduce_fusion.1
  48.9 2.1 convolution_bitcast_fusion.6
  50.9 1.2 multiply_convert_fusion.1
  52.2 0.9 fusion.20
  53.1 2.1 multiply_reduce_fusion.3
  55.2 2.1 convolution_bitcast_fusion.8
  57.3 1.2 multiply_convert_fusion.3
  58.5 0.9 fusion.18
  59.5 2.1 multiply_reduce_fusion
  61.6 1.4 convolution_bitcast_fusion.5
  63.2 0.8 copy-done.32
  64.3 0.7 copy-done.8
  66.2 0.8 pad_maximum_fusion.1
  67.0 14.2 %fusion.90 = (f32[56,512]{1,0:T(8,128)S(1)}, f32[56,512]{1,0:T(8,128)}) fusion(f32[200,512]{1,0:T(8,128)S(1)} %pad_maximum_fusion.4, f32[200,512]{1,0:T(8,128)} %pad_maximum_fusion.1), kind=kCustom, calls=%all-reduce-scatter.2 | all-reduce-scatter fusion | flops 229377 | bytes 1049088
  81.3 1.4 slice.107
  82.7 1.3 collective-permute-start.1
  84.0 0.6 slice.106
  84.6 1.3 collective-permute-start
  85.9 0.9 fusion.15
  86.8 0.9 fusion.16
  88.0 0.6 copy-done.38
  88.9 0.7 copy-done.10
  89.7 0.9 copy-done.27
  90.7 0.8 copy-done.28
  91.9 0.8 pad_maximum_fusion
  93.2 0.7 copy-done.43
  95.2 0.9 concatenate.45
  96.1 0.9 concatenate.44
  97.2 1.0 add.33
  98.1 1.0 add.32
  99.1 0.7 convert_bitcast_fusion
  99.8 0.7 convert_bitcast_fusion.1
  101.3 49.4 %psum.15 = f32[16,512]{1,0:T(8,128)S(1)} all-reduce(f32[16,512]{1,0:T(8,128)S(1)} %fusion.22), channel_id=1, replica_groups=mesh['dp'=8,'ctx'=4] {'dp','ctx'}, use_global_device_ids=true, to_apply=%region_11.12 | all-reduce | flops 8192 | bytes 65536 | tf_op jit(solution)/shard_map/psum | solution.py:129
  150.8 1.2 convolution_bitcast_fusion
  152.0 0.6 broadcast_multiply_fusion.1
  152.6 124.1 %all-reduce.7.cloned.1.call-done = f32[4096,16]{0,1:T(8,128)} async-done(((f32[4096,16]{0,1:T(8,128)}), f32[4096,16]{0,1:T(8,128)}) %all-reduce.7.cloned.1.call-update) | async-done | bytes 262160 | tf_op jit(solution)/shard_map/psum | solution.py:129
  276.7 1.7 broadcast_multiply_fusion
  (115 shorter events, 7.5 us)
Async XLA Ops:
  7.2 93.3 %copy-start = (bf16[1,1,128,4096]{3,2,1,0:T(8,128)(2,1)S(1)}, bf16[1,1,128,4096]{3,2,1,0:T(8,128)(2,1)}, u32[]{:S(2)}) copy-start(bf16[1,1,128,4096]{3,2,1,0:T(8,128)(2,1)} %param.12) | copy-start | bytes 3145732
  7.2 269.5 %all-reduce.7.cloned.1.call-start = ((), (), s32[]{:S(2)}) async-start(), calls=%async_computation | async-start | bytes 524288 | tf_op jit(solution)/shard_map/psum | solution.py:129
  8.1 1.0 copy-start.6
  21.0 12.9 %copy-start.29 = (bf16[1,1,128,2048]{3,2,1,0:T(8,128)(2,1)S(1)}, bf16[1,1,128,2048]{3,2,1,0:T(8,128)(2,1)}, u32[]{:S(2)}) copy-start(bf16[1,1,128,2048]{3,2,1,0:T(8,128)(2,1)} %param.8) | copy-start | bytes 1572868
  34.1 1.2 copy-start.30
  35.7 0.6 copy-start.23
  35.7 2.0 copy-start.24
  36.6 16.5 %copy-start.1 = (f32[4,128,328]{1,2,0:T(8,128)}, f32[4,128,328]{1,2,0:T(8,128)S(1)}, u32[]{:S(2)}) copy-start(f32[4,128,328]{1,2,0:T(8,128)S(1)} %convolution_bitcast_fusion.4) | copy-start | bytes 2015236
  37.7 1.2 copy-start.7
  39.0 7.6 %copy-start.40 = (pred[128,328]{0,1:T(8,128)(4,1)}, pred[128,328]{0,1:T(8,128)(4,1)S(1)}, u32[]{:S(2)}) copy-start(pred[128,328]{0,1:T(8,128)(4,1)S(1)} %pad_add_fusion) | copy-start | bytes 125956
  39.0 0.9 copy-start.36
  39.9 2.3 copy-start.25
  42.3 2.1 copy-start.4
  44.4 1.2 copy-start.37
  45.6 0.9 copy-start.34
  48.9 2.1 copy-start.3
  50.9 1.2 copy-start.35
  55.2 2.1 copy-start.2
  57.3 1.2 copy-start.33
  58.5 0.9 copy-start.31
  58.5 0.9 copy-start.41
  61.6 1.4 copy-start.5
  63.0 2.1 copy-start.21
  63.1 1.0 copy-start.32
  64.0 0.9 copy-start.8
  64.0 1.0 copy-start.9
  64.0 1.1 copy-start.11
  65.1 0.7 copy-start.13
  65.1 1.0 copy-start.15
  65.1 1.1 copy-start.17
  65.1 1.1 copy-start.19
  82.7 12.5 %collective-permute-start.1 = (f32[18,512]{1,0:T(8,128)}, f32[18,512]{1,0:T(8,128)}, u32[]{:S(2)}, u32[]{:S(2)}) collective-permute-start(f32[18,512]{1,0:T(8,128)} %slice.107), channel_id=1, source_target_pairs={{0,1},{1,2},{2,3},{4,5},{5,6},{6,7},{8,9},{9,10},{10,11},{12,13},{... | collective-permute-start | bytes 110600
  84.6 11.5 %collective-permute-start = (f32[18,512]{1,0:T(8,128)}, f32[18,512]{1,0:T(8,128)}, u32[]{:S(2)}, u32[]{:S(2)}) collective-permute-start(f32[18,512]{1,0:T(8,128)} %slice.106), channel_id=1, source_target_pairs={{0,1},{1,2},{2,3},{4,5},{5,6},{6,7},{8,9},{9,10},{10,11},{12,13},{... | collective-permute-start | bytes 110600
  87.7 0.9 copy-start.38
  88.6 0.9 copy-start.10
  88.6 1.0 copy-start.12
  88.6 1.1 copy-start.14
  89.7 0.9 copy-start.27
  90.6 0.9 copy-start.28
  91.8 0.9 copy-start.16
  91.9 1.1 copy-start.18
  91.9 1.3 copy-start.20
  91.9 1.3 copy-start.22
  93.2 2.0 copy-start.26
  93.2 0.7 copy-start.43
  99.8 1.0 copy-start.39
  101.3 49.5 %copy-start.42 = (bf16[16,512]{1,0:T(8,128)(2,1)S(1)}, bf16[16,512]{1,0:T(8,128)(2,1)}, u32[]{:S(2)}) copy-start(bf16[16,512]{1,0:T(8,128)(2,1)} %param.14) | copy-start | bytes 49156
Sparse Core Ops, SparseCore 0:
  152.1 124.5 all-reduce.6
where the time goes:
time: 291 us; the launch traced here: 285 us
  waiting for transfers between devices  124 us (43%)
  blocking collectives  88.3 us (30%)
  matrix products  26.3 us (9%)
  local copies, waits for them, and re-layouts  18 us (6%)
  between operations  16 us (5%)
  other arithmetic  10 us (3%)
    psum x1, waiting for transfers between devices, per_device(): lax.psum(adapter_terms(hidden_row_block, low_rank_rows, value_result, ada...  124 us
    psum x1, blocking collectives, per_device(): lax.psum(adapter_terms(hidden_row_block, low_rank_rows, value_result, ada...  49.4 us
    unnamed x1, blocking collectives  14.2 us
    unnamed x99, local copies, waits for them, and re-layouts  13.8 us
    all_gather x1, blocking collectives, per_device(): lax.all_gather(own_keys, 'ctx', axis=0, tiled=True)  12.8 us
    all_gather x1, blocking collectives, per_device(): lax.all_gather(own_values, 'ctx', axis=0, tiled=True)  11.7 us
    div x4, matrix products, group_grads(): attend = unnorm / jnp.sum(unnorm, -1, keepdims=True)  8.94 us
    dot_general x4, matrix products, group_grads(): jnp.einsum('gtm,tgd->md', attend_low, cot_group, preferred_element_type=j...  7.65 us
  transfers between devices with their start and end apart: 3, of which 1 were waited for; matrix products, arithmetic and copies ran while one was open for 2% of the time, Pallas kernels for 0%

commit v1 on v0

v1 whole, which is shorter than its diff:
```python
import functools
import math

import jax
import jax.numpy as jnp
from jax import lax
from jax.experimental import pallas as pl
from jax.experimental.pallas import tpu as pltpu
from jax.sharding import PartitionSpec as P

HEAD_SIZE = 128
SUMM = 50
SLOT = 64
BACK = 104
ADAPTER_SCALE = 2.0
MESH = pl.DeviceIdType.MESH
F32 = jnp.float32
BF16 = jnp.bfloat16


def iota(shape, dim):
    return lax.broadcasted_iota(jnp.int32, shape, dim)


def dot(a, b, ca=1, cb=0):
    return lax.dot_general(a, b, (((ca,), (cb,)), ((), ())), preferred_element_type=F32)


def kernel(
    ndp, nctx, kv, groups, tokens, ups_each,
    len_ref, k_hbm, v_hbm, wt_hbm, up_hbm, q_hbm, cot_hbm, hid_hbm,
    gq_hbm, gk_hbm, gv_hbm, down_hbm, upg_hbm,
    gq_ref, gk_ref, gv_ref, down_ref, upg_ref,
    k_ref, v_ref, wt_ref, up_ref, q_ref, cot_ref, hid_ref, hx, bx, own, mem, loc, rcv, mask_ref, s_ref, dp_ref, p_ref, ds_ref,
    pay, rs, zbuf, gat,
    load_sem, store_sem, fs_sem, fr_sem, bs_sem, br_sem, s0, r0, sb, rb, s1, r1, s2, r2, s3, r3,
):
    D = HEAD_SIZE
    nmem = nctx * SLOT
    scale = 1.0 / math.sqrt(D)
    dp = lax.axis_index("dp")
    me = lax.axis_index("ctx")
    loads = [
        pltpu.make_async_copy(src, dst, load_sem.at[i])
        for i, (src, dst) in enumerate((
            (k_hbm, k_ref), (v_hbm, v_ref), (hid_hbm, hid_ref), (wt_hbm, wt_ref),
            (q_hbm, q_ref), (cot_hbm, cot_ref), (up_hbm, up_ref)))
    ]
    for c in loads:
        c.start()
    stores = [
        pltpu.make_async_copy(src, dst, store_sem.at[i])
        for i, (src, dst) in enumerate((
            (gq_ref, gq_hbm), (gk_ref, gk_hbm), (gv_ref, gv_hbm), (down_ref, down_hbm), (upg_ref, upg_hbm)))
    ]

    mem[...] = jnp.zeros_like(mem)
    rcv[...] = jnp.zeros_like(rcv)

    barrier = pltpu.get_barrier_semaphore()
    for k in range(1, ndp):
        pl.semaphore_signal(barrier, inc=1, device_id=(lax.rem(dp + k, ndp), me), device_id_type=MESH)
    for k in range(1, nctx):
        pl.semaphore_signal(barrier, inc=1, device_id=(dp, lax.rem(me + k, nctx)), device_id_type=MESH)

    loads[0].wait()
    loads[1].wait()
    length = len_ref[0, 0]
    live = length + SUMM
    r = iota((SLOT, tokens), 0)
    pick = jnp.where((iota((SLOT, tokens), 1) == length + r) & (r < SUMM), 1.0, 0.0).astype(BF16)
    own_k = dot(pick, k_ref[...]).astype(BF16)
    own_v = dot(pick, v_ref[...]).astype(BF16)
    for h in range(kv):
        own[h, 0:SLOT, :] = own_k[:, h * D:(h + 1) * D]
        own[h, SLOT:2 * SLOT, :] = own_v[:, h * D:(h + 1) * D]

    i = iota((nmem, tokens), 0)
    mask_ref[0:nmem, :] = jnp.where(((i >> 6) < me) & ((i & 63) < SUMM), 1.0, 0.0)
    p = iota((tokens, tokens), 0)
    t = iota((tokens, tokens), 1)
    mask_ref[nmem:nmem + tokens, :] = jnp.where((p <= t) & (p < live), 1.0, 0.0)

    pl.semaphore_wait(barrier, ndp - 1 + nctx - 1)

    def forward(h, k):
        return pltpu.make_async_remote_copy(
            src_ref=own.at[h], dst_ref=mem.at[h, me],
            send_sem=fs_sem.at[h, k], recv_sem=fr_sem.at[h, k],
            device_id=(dp, lax.rem(me + k, nctx)), device_id_type=MESH)

    for h in range(kv):
        for k in range(1, nctx):
            @pl.when(me + k < nctx)
            def _():
                forward(h, k).start()

    chunk = hid_ref.shape[1] // ndp
    loads[2].wait()

    def columns(d):
        return pl.ds(pl.multiple_of(d * chunk, 128), chunk)

    def exchange(k):
        to = lax.rem(dp + k, ndp)
        return pltpu.make_async_remote_copy(
            src_ref=hid_ref.at[:, columns(to)], dst_ref=hx.at[k], send_sem=s0.at[k], recv_sem=r0.at[k],
            device_id=(to, me), device_id_type=MESH)

    for k in range(1, ndp):
        exchange(k).start()

    loads[3].wait()
    low = dot(hid_ref[...], wt_ref[...], 1, 1).astype(BF16)
    loads[4].wait()
    loads[5].wait()
    loads[6].wait()
    row = iota((tokens, D), 0)
    cot_mask = jnp.where(row < live, 1.0, 0.0).astype(BF16)

    def backward(h, j):
        return pltpu.make_async_remote_copy(
            src_ref=loc.at[h, j, pl.ds(0, BACK)], dst_ref=rcv.at[h, j, pl.ds(0, BACK)],
            send_sem=bs_sem.at[h, j], recv_sem=br_sem.at[h, j],
            device_id=(dp, lax.max(me - 1, 0)), device_id_type=MESH)

    def chain(h):
        for j in range(nctx - 1):
            @pl.when((me < nctx - 1) & (j <= me))
            def _():
                backward(h, j).wait_recv()

            @pl.when((me < nctx - 1) & (j < me))
            def _():
                loc[h, j, 0:BACK, :] = loc[h, j, 0:BACK, :] + rcv[h, j, 0:BACK, :]
                backward(h, j).start()

    pr = iota((tokens, 128), 0) - length
    cr = iota((tokens, 128), 1)
    put_k = jnp.where((pr == cr) & (cr < SUMM), 1.0, 0.0).astype(BF16)
    put_v = jnp.where((pr == cr - SUMM) & (pr >= 0) & (pr < SUMM), 1.0, 0.0).astype(BF16)
    key_parts, value_parts = [], []

    def finish(h, back_sum):
        cols = slice(h * D, (h + 1) * D)
        back = rcv[h, me, :, :]
        hi = back.astype(BF16)
        rest = back - hi.astype(F32)
        mid = rest.astype(BF16)
        lo = (rest - mid.astype(F32)).astype(BF16)
        gv = (value_parts[h] + ((dot(put_v, lo) + dot(put_v, mid)) + dot(put_v, hi))).astype(BF16)
        gv_ref[:, cols] = gv
        back_sum = back_sum + dot(up_ref[:, cols], gv, 1, 1)
        gk = key_parts[h] + ((dot(put_k, lo) + dot(put_k, mid)) + dot(put_k, hi))
        gk_ref[:, cols] = gk.astype(BF16)
        up_part = dot(low, gv, 0, 0)
        for a in range(rank // 8):
            n = a * kv + h
            at = (n % ups_each) * 8
            pay[n // ups_each, at:at + 8, :] = up_part[a * 8:a * 8 + 8]
        return back_sum

    rank = up_ref.shape[0]
    back_sum = jnp.zeros((rank, tokens), F32)
    for n in range(rank // 8 * kv, ndp * ups_each):
        at = (n % ups_each) * 8
        pay[n // ups_each, at:at + 8, :] = jnp.zeros((8, 128), F32)

    for h in range(kv):
        for k in range(1, nctx):
            @pl.when(me >= k)
            def _():
                forward(h, k).wait_recv()
        cols = slice(h * D, (h + 1) * D)
        keys = jnp.concatenate([mem[h, j, 0:SLOT, :] for j in range(nctx)] + [k_ref[:, cols]], 0)
        vals = jnp.concatenate([mem[h, j, SLOT:2 * SLOT, :] for j in range(nctx)] + [v_ref[:, cols]], 0)
        heads = [h * groups + g for g in range(groups)]
        q = jnp.concatenate([q_ref[:, a * D:(a + 1) * D] for a in heads], 0)
        c = jnp.concatenate([cot_ref[:, a * D:(a + 1) * D] * cot_mask for a in heads], 0)
        s_ref[...] = dot(keys, q, 1, 1)
        dp_ref[...] = dot(vals, c, 1, 1)
        for g in range(groups):
            lanes = slice(g * tokens, (g + 1) * tokens)
            e = jnp.exp(s_ref[:, lanes] * scale) * mask_ref[...]
            attend = e * (1.0 / jnp.sum(e, 0, keepdims=True))
            grad = dp_ref[:, lanes]
            dot_row = jnp.sum(attend * grad, 0, keepdims=True)
            p_ref[:, lanes] = attend.astype(BF16)
            ds_ref[:, lanes] = (attend * (grad - dot_row)).astype(BF16)
        ds = ds_ref[...]
        dk = dot(ds, q) * scale
        dv = dot(p_ref[...], c)
        for j in range(nctx - 1):
            at = j * SLOT
            tail = pltpu.roll(dv[at:at + SLOT], 2, 0)
            loc[h, j, 0:48, :] = dk[at:at + 48]
            loc[h, j, 48:56, :] = dk[at + 48:at + 56] + tail[0:8]
            loc[h, j, 56:BACK, :] = tail[8:56]

            @pl.when(me == nctx - 1)
            def _():
                backward(h, j).start()
        key_parts.append(dk[nmem:])
        value_parts.append(dv[nmem:])
        dq = dot(ds, keys, 0, 0) * scale
        for g, a in enumerate(heads):
            gq_ref[:, a * D:(a + 1) * D] = dq[g * tokens:(g + 1) * tokens].astype(BF16)
        if h > 0:
            chain(h - 1)
            back_sum = finish(h - 1, back_sum)
    stores[0].start()
    chain(kv - 1)
    back_sum = finish(kv - 1, back_sum)

    bx[0] = back_sum.astype(BF16)

    def tell(k):
        return pltpu.make_async_remote_copy(
            src_ref=bx.at[0], dst_ref=bx.at[k], send_sem=sb.at[k], recv_sem=rb.at[k],
            device_id=(lax.rem(dp + k, ndp), me), device_id_type=MESH)

    def scatter(k):
        to = lax.rem(dp + k, ndp)
        return pltpu.make_async_remote_copy(
            src_ref=pay.at[to], dst_ref=rs.at[k], send_sem=s1.at[k], recv_sem=r1.at[k],
            device_id=(to, me), device_id_type=MESH)

    def spread(k):
        return pltpu.make_async_remote_copy(
            src_ref=zbuf.at[me], dst_ref=zbuf.at[me], send_sem=s2.at[k], recv_sem=r2.at[k],
            device_id=(dp, lax.rem(me + k, nctx)), device_id_type=MESH)

    def spread_in(k):
        come = lax.rem(me + nctx - k, nctx)
        return pltpu.make_async_remote_copy(
            src_ref=zbuf.at[come], dst_ref=zbuf.at[come], send_sem=s2.at[k], recv_sem=r2.at[k],
            device_id=(dp, come), device_id_type=MESH)

    def gather(k):
        return pltpu.make_async_remote_copy(
            src_ref=gat.at[dp], dst_ref=gat.at[dp], send_sem=s3.at[k], recv_sem=r3.at[k],
            device_id=(lax.rem(dp + k, ndp), me), device_id_type=MESH)

    def gather_in(k):
        come = lax.rem(dp + ndp - k, ndp)
        return pltpu.make_async_remote_copy(
            src_ref=gat.at[come], dst_ref=gat.at[come], send_sem=s3.at[k], recv_sem=r3.at[k],
            device_id=(come, me), device_id_type=MESH)

    for k in range(1, ndp):
        tell(k).start()
    for k in range(1, ndp):
        scatter(k).start()
    stores[1].start()
    stores[2].start()
    down = dot(bx[0], hid_ref[:, columns(dp)])
    up_sum = pay[dp]
    for k in range(1, ndp):
        exchange(k).wait_recv()
        tell(k).wait_recv()
        down = down + dot(bx[k], hx[k])
    for k in range(1, ndp):
        scatter(k).wait_recv()
        up_sum = up_sum + rs[k]
    blocks = chunk // 128
    for b in range(blocks):
        zbuf[me, b * rank:(b + 1) * rank, :] = down[:, b * 128:(b + 1) * 128]
    zbuf[me, blocks * rank:blocks * rank + ups_each * 8, :] = up_sum
    for k in range(1, nctx):
        spread(k).start()
    for k in range(1, nctx):
        spread_in(k).wait_recv()
    total = zbuf[0]
    for j in range(1, nctx):
        total = total + zbuf[j]
    gat[dp] = total * (ADAPTER_SCALE / (ndp * nctx))
    for k in range(1, ndp):
        gather(k).start()
    for d in range(ndp):
        if d < ndp - 1:
            gather_in(d + 1).wait_recv()
    for d in range(ndp):
        for b in range(blocks):
            at = d * chunk + b * 128
            down_ref[:, at:at + 128] = gat[d, b * rank:(b + 1) * rank, :]
        for u in range(ups_each):
            n = d * ups_each + u
            if n < rank // 8 * kv:
                at = blocks * rank + u * 8
                a, b = n // kv * 8, n % kv * 128
                upg_ref[a:a + 8, b:b + 128] = gat[d, at:at + 8, :]

    stores[3].start()
    stores[4].start()

    for h in range(kv):
        for k in range(1, nctx):
            @pl.when(me + k < nctx)
            def _():
                forward(h, k).wait_send()
        for j in range(nctx - 1):
            @pl.when(j < me)
            def _():
                backward(h, j).wait_send()
    for k in range(1, ndp):
        exchange(k).wait_send()
        tell(k).wait_send()
        scatter(k).wait_send()
        gather(k).wait_send()
    for k in range(1, nctx):
        spread(k).wait_send()
    for c in stores:
        c.wait()


def write_out(*refs):
    sems = refs[10]
    copies = [pltpu.make_async_copy(refs[i], refs[i + 5], sems.at[i]) for i in range(5)]
    for c in copies:
        c.start()
    for c in copies:
        c.wait()


def per_device(ndp, nctx, queries, rotated_key_rows, values, cotangent, hidden, down_w, up_w, seg_len):
    q, k, v, cot, hid = (a[0, 0] for a in (queries, rotated_key_rows, values, cotangent, hidden))
    tokens, width = k.shape
    kv = width // HEAD_SIZE
    groups = q.shape[1] // width
    model = hid.shape[1]
    rank = up_w.shape[0]
    D = HEAD_SIZE
    ups_each = -(-(rank // 8 * kv) // ndp)
    chunk = model // ndp
    rows = chunk // 128 * rank + ups_each * 8
    nkeys = nctx * SLOT + tokens
    lanes = groups * tokens
    hbm = pl.BlockSpec(memory_space=pl.ANY)
    sm = pl.BlockSpec(memory_space=pltpu.SMEM)
    dma = pltpu.SemaphoreType.DMA
    results = pl.pallas_call(
        functools.partial(kernel, ndp, nctx, kv, groups, tokens, ups_each),
        out_shape=(
            jax.ShapeDtypeStruct(q.shape, BF16),
            jax.ShapeDtypeStruct(k.shape, BF16),
            jax.ShapeDtypeStruct(v.shape, BF16),
            jax.ShapeDtypeStruct((rank, model), F32),
            jax.ShapeDtypeStruct((rank, width), F32),
        ),
        in_specs=[sm] + [hbm] * 7,
        out_specs=(hbm,) * 5,
        scratch_shapes=[
            pltpu.VMEM(q.shape, BF16),
            pltpu.VMEM(k.shape, BF16),
            pltpu.VMEM(v.shape, BF16),
            pltpu.VMEM((rank, model), F32),
            pltpu.VMEM((rank, width), F32),
            pltpu.VMEM(k.shape, BF16),
            pltpu.VMEM(v.shape, BF16),
            pltpu.VMEM((rank, model), BF16),
            pltpu.VMEM((rank, width), BF16),
            pltpu.VMEM(q.shape, BF16),
            pltpu.VMEM(cot.shape, BF16),
            pltpu.VMEM(hid.shape, BF16),
            pltpu.VMEM((ndp, tokens, chunk), BF16),
            pltpu.VMEM((ndp, rank, tokens), BF16),
            pltpu.VMEM((kv, 2 * SLOT, D), BF16),
            pltpu.VMEM((kv, nctx, 2 * SLOT, D), BF16),
            pltpu.VMEM((kv, nctx, 128, D), F32),
            pltpu.VMEM((kv, nctx, 128, D), F32),
            pltpu.VMEM((nkeys, tokens), F32),
            pltpu.VMEM((nkeys, lanes), F32),
            pltpu.VMEM((nkeys, lanes), F32),
            pltpu.VMEM((nkeys, lanes), BF16),
            pltpu.VMEM((nkeys, lanes), BF16),
            pltpu.VMEM((ndp, ups_each * 8, 128), F32),
            pltpu.VMEM((ndp, ups_each * 8, 128), F32),
            pltpu.VMEM((nctx, rows, 128), F32),
            pltpu.VMEM((ndp, rows, 128), F32),
            dma((7,)), dma((5,)),
            dma((kv, nctx)), dma((kv, nctx)),
            dma((kv, nctx)), dma((kv, nctx)),
            dma((ndp,)), dma((ndp,)),
            dma((ndp,)), dma((ndp,)),
            dma((ndp,)), dma((ndp,)),
            dma((nctx,)), dma((nctx,)),
            dma((ndp,)), dma((ndp,)),
        ],
        compiler_params=pltpu.CompilerParams(
            collective_id=0, has_side_effects=True, vmem_limit_bytes=62 * 1024 * 1024),
    )(seg_len, k, v, down_w.T, up_w, q, cot, hid)
    gq, gk, gv, down, upg = pl.pallas_call(
        write_out,
        out_shape=tuple(jax.ShapeDtypeStruct(a.shape, a.dtype) for a in results),
        in_specs=[hbm] * 5,
        out_specs=(hbm,) * 5,
        scratch_shapes=[dma((5,))],
        compiler_params=pltpu.CompilerParams(vmem_limit_bytes=62 * 1024 * 1024),
    )(*results)
    return gq[None, None], gk[None, None], gv[None, None], down.T, upg


def solution(mesh):
    split = P("dp", "ctx", None, None)
    return jax.shard_map(
        functools.partial(per_device, mesh.shape["dp"], mesh.shape["ctx"]),
        mesh=mesh,
        in_specs=(split,) * 5 + (P(), P(), P("dp", "ctx")),
        out_specs=(split,) * 3 + (P(), P()),
        check_vma=False,
    )
```

time: 291 us -> 81 us (0.28); the launches traced: 285 us -> 80.9 us
  waiting for transfers between devices: 124 us -> 0 us
  blocking collectives: 88.3 us -> 0 us
  Pallas kernels: 0 us -> 79.6 us
  matrix products: 26.3 us -> 0 us
  local copies, waits for them, and re-layouts: 18 us -> 0 us
  between operations: 16 us -> 1.29 us
  other arithmetic: 10 us -> 0 us
    psum x1 -> x0, waiting for transfers between devices: 124 us -> none  [per_device(): lax.psum(adapter_terms(hidden_row_block, low_rank_rows, value_result, ada...]
    pallas_call x0 -> x2, Pallas kernels: none -> 79.6 us  [the longest x1 45.7 us: per_device(): pl.pallas_call(functools.partial(kernel, ndp, nctx, kv, groups, tokens, u...]
    psum x1 -> x0, blocking collectives: 49.4 us -> none  [per_device(): lax.psum(adapter_terms(hidden_row_block, low_rank_rows, value_result, ada...]
    all_gather x2 -> x0, blocking collectives: 24.6 us -> none  [the longest x1 12.8 us: per_device(): lax.all_gather(own_keys, 'ctx', axis=0, tiled=True)]
    dot_general x18 -> x0, matrix products: 17.3 us -> none  [the longest x4 7.65 us: group_grads(): jnp.einsum('gtm,tgd->md', attend_low, cot_group, preferred_element_type=j...]
    unnamed x1 -> x0, blocking collectives: 14.2 us -> none
    unnamed x99 -> x0, local copies, waits for them, and re-layouts: 13.8 us -> none
    div x4 -> x0, matrix products: 8.94 us -> none  [group_grads(): attend = unnorm / jnp.sum(unnorm, -1, keepdims=True)]
  transfers between devices with their start and end apart: 3 -> 0, of which waited for: 1 -> 0; matrix products, arithmetic and copies ran while one was open for 2% -> 0% of each run, Pallas kernels for 0% -> 0%
where the time goes in v1:
time: 81 us; the launch traced here: 80.9 us
  Pallas kernels  79.6 us (98%)
  between operations  1.29 us (2%)
    pallas_call x1, Pallas kernels, per_device(): pl.pallas_call(functools.partial(kernel, ndp, nctx, kv, groups, tokens, u...  45.7 us
    pallas_call x1, Pallas kernels, per_device(): pl.pallas_call(write_out, out_shape=tuple((jax.ShapeDtypeStruct(a.shape,...  33.9 us

profile of v1, /device:TPU:25, one launch (start us, length us, event | category | flops | bytes accessed | tf_op | source)
XLA Modules:
  0.0 80.9 jit_solution(17932704733969118141)
XLA Ops:
  1.3 45.7 %shard_map.119 = (bf16[128,2048]{1,0:T(8,128)(2,1)}, bf16[128,512]{1,0:T(8,128)(2,1)}, bf16[128,512]{1,0:T(8,128)(2,1)}, f32[16,4096]{1,0:T(8,128)}, f32[16,512]{1,0:T(8,128)}) custom-call(s32[1,1]{1,0:T(1,128)S(6)} %copy.13.len_ref, bf16[128,512]{1,0:T(8,128)(2,1)} %bitcast.13, bf16[128,512]{1,0:T(8,128)(2,1)} %bitcast.14, bf16[16,4096]{1,0:T(8,128)(2,1)} %bitcast.15, ...), custom_call_target="tpu_custom_call" | custom-call | tf_op jit(solution)/shard_map/pallas_call | solution.py:341
  46.9 33.9 %shard_map.120 = (bf16[128,2048]{1,0:T(8,128)(2,1)}, bf16[128,512]{1,0:T(8,128)(2,1)}, bf16[128,512]{1,0:T(8,128)(2,1)}, f32[16,4096]{1,0:T(8,128)}, f32[16,512]{1,0:T(8,128)}) custom-call(bf16[128,2048]{1,0:T(8,128)(2,1)} %get-tuple-element.15.refs_0_, bf16[128,512]{1,0:T(8,128)(2,1)} %get-tuple-element.16.refs_1_, ...), custom_call_target="tpu_custom_call" | custom-call | tf_op jit(solution)/shard_map/pallas_call | solution.py:392

commit v2 on v1

--- a/solution.py
+++ b/solution.py
@@ -314,11 +314,15 @@
 
 
 def write_out(*refs):
-    sems = refs[10]
-    copies = [pltpu.make_async_copy(refs[i], refs[i + 5], sems.at[i]) for i in range(5)]
-    for c in copies:
+    ins, outs, held, sem_in, sem_out = refs[:5], refs[5:10], refs[10:15], refs[15], refs[16]
+    loads = [pltpu.make_async_copy(ins[i], held[i], sem_in.at[i]) for i in range(5)]
+    stores = [pltpu.make_async_copy(held[i], outs[i], sem_out.at[i]) for i in range(5)]
+    for c in loads:
         c.start()
-    for c in copies:
+    for i in range(5):
+        loads[i].wait()
+        stores[i].start()
+    for c in stores:
         c.wait()
 
 
@@ -394,7 +398,7 @@
         out_shape=tuple(jax.ShapeDtypeStruct(a.shape, a.dtype) for a in results),
         in_specs=[hbm] * 5,
         out_specs=(hbm,) * 5,
-        scratch_shapes=[dma((5,))],
+        scratch_shapes=[pltpu.VMEM(a.shape, a.dtype) for a in results] + [dma((5,)), dma((5,))],
         compiler_params=pltpu.CompilerParams(vmem_limit_bytes=62 * 1024 * 1024),
     )(*results)
     return gq[None, None], gk[None, None], gv[None, None], down.T, upg

time: 81 us -> 49.2 us (0.61)
  Pallas kernels: 79.6 us -> 47.8 us
    pallas_call x1, Pallas kernels: 33.9 us -> 2.09 us  [per_device(): pl.pallas_call(write_out, out_shape=tuple((jax.ShapeDtypeStruct(a.shape,...]
where the time goes in v2:
time: 49.2 us; the launch traced here: 49 us
  Pallas kernels  47.8 us (97%)
  between operations  1.29 us (3%)
    pallas_call x1, Pallas kernels, per_device(): pl.pallas_call(functools.partial(kernel, ndp, nctx, kv, groups, tokens, u...  45.7 us
    pallas_call x1, Pallas kernels, per_device(): pl.pallas_call(write_out, out_shape=tuple((jax.ShapeDtypeStruct(a.shape,...  2.09 us

profile of v2, /device:TPU:25, one launch (start us, length us, event | category | flops | bytes accessed | tf_op | source)
XLA Modules:
  0.0 49.0 jit_solution(4025441031722675814)
XLA Ops:
  1.3 45.7 %shard_map.119 = (bf16[128,2048]{1,0:T(8,128)(2,1)}, bf16[128,512]{1,0:T(8,128)(2,1)}, bf16[128,512]{1,0:T(8,128)(2,1)}, f32[16,4096]{1,0:T(8,128)}, f32[16,512]{1,0:T(8,128)}) custom-call(s32[1,1]{1,0:T(1,128)S(6)} %copy.13.len_ref, bf16[128,512]{1,0:T(8,128)(2,1)} %bitcast.13, bf16[128,512]{1,0:T(8,128)(2,1)} %bitcast.14, bf16[16,4096]{1,0:T(8,128)(2,1)} %bitcast.15, ...), custom_call_target="tpu_custom_call" | custom-call | tf_op jit(solution)/shard_map/pallas_call | solution.py:345
  46.9 2.1 %shard_map.120 = (bf16[128,2048]{1,0:T(8,128)(2,1)}, bf16[128,512]{1,0:T(8,128)(2,1)}, bf16[128,512]{1,0:T(8,128)(2,1)}, f32[16,4096]{1,0:T(8,128)}, f32[16,512]{1,0:T(8,128)}) custom-call(bf16[128,2048]{1,0:T(8,128)(2,1)} %get-tuple-element.15.refs_0_, bf16[128,512]{1,0:T(8,128)(2,1)} %get-tuple-element.16.refs_1_, ...), custom_call_target="tpu_custom_call" | custom-call | tf_op jit(solution)/shard_map/pallas_call | solution.py:396

commit v3 on v2

--- a/solution.py
+++ b/solution.py
@@ -11,7 +11,9 @@
 HEAD_SIZE = 128
 SUMM = 50
 SLOT = 64
-BACK = 104
+BACK = 112
+STEPS = 64.0
+TOP = 32000.0
 ADAPTER_SCALE = 2.0
 MESH = pl.DeviceIdType.MESH
 F32 = jnp.float32
@@ -24,6 +26,60 @@
 
 def dot(a, b, ca=1, cb=0):
     return lax.dot_general(a, b, (((ca,), (cb,)), ((), ())), preferred_element_type=F32)
+
+
+def code(x):
+    most = jnp.max(jnp.abs(x), 0, keepdims=True)
+    level = jnp.ceil(jnp.log(jnp.maximum(most, 1e-30)) * (STEPS / math.log(2.0))) + 1.0
+    return jnp.round(x * (TOP * jnp.exp(level * (-math.log(2.0) / STEPS)))), level
+
+
+def scale_of(level):
+    return jnp.exp(level * (math.log(2.0) / STEPS)) * (1.0 / TOP)
+
+
+def level_rows(first, second, rows):
+    at = iota((rows, 128), 0)
+    return jnp.where(at == 0, first, jnp.where(at == 1, second, 0.0))
+
+
+def to_wire(x):
+    return x.astype(jnp.int32).astype(jnp.int16)
+
+
+def from_wire(x):
+    return x.astype(jnp.int32).astype(F32)
+
+
+def pack_terms(both):
+    k, level_k = code(both[0:SLOT])
+    v, level_v = code(both[SLOT:2 * SLOT])
+    v = pltpu.roll(v, 2, 0)
+    return to_wire(jnp.concatenate(
+        [k[0:48], k[48:56] + v[0:8], v[8:56], level_rows(level_k, level_v, 8)], 0))
+
+
+def unpack_terms(wire):
+    x = from_wire(wire)
+    keep = iota((SLOT, 128), 0) < SUMM
+    k = jnp.where(keep, x[0:SLOT] * scale_of(x[104:105]), 0.0)
+    v = jnp.where(keep, pltpu.roll(x[48:112], SLOT - 2, 0) * scale_of(x[105:106]), 0.0)
+    return jnp.concatenate([k, v], 0)
+
+
+def pack_sums(x, first):
+    a, level_a = code(x[:first])
+    b, level_b = code(x[first:])
+    wire = [a, b, level_rows(level_a, level_b, 8)]
+    if (x.shape[0] + 8) % 16:
+        wire.append(jnp.zeros((8, 128), F32))
+    return to_wire(jnp.concatenate(wire, 0))
+
+
+def unpack_sums(wire, first, rows):
+    x = from_wire(wire)
+    return jnp.concatenate(
+        [x[:first] * scale_of(x[rows:rows + 1]), x[first:rows] * scale_of(x[rows + 1:rows + 2])], 0)
 
 
 def kernel(
@@ -31,7 +87,7 @@
     len_ref, k_hbm, v_hbm, wt_hbm, up_hbm, q_hbm, cot_hbm, hid_hbm,
     gq_hbm, gk_hbm, gv_hbm, down_hbm, upg_hbm,
     gq_ref, gk_ref, gv_ref, down_ref, upg_ref,
-    k_ref, v_ref, wt_ref, up_ref, q_ref, cot_ref, hid_ref, hx, bx, own, mem, loc, rcv, mask_ref, s_ref, dp_ref, p_ref, ds_ref,
+    k_ref, v_ref, wt_ref, up_ref, q_ref, cot_ref, hid_ref, hx, bx, own, mem, loc, out, rcv, mask_ref, s_ref, dp_ref, p_ref, ds_ref,
     pay, rs, zbuf, gat,
     load_sem, store_sem, fs_sem, fr_sem, bs_sem, br_sem, s0, r0, sb, rb, s1, r1, s2, r2, s3, r3,
 ):
@@ -120,7 +176,7 @@
 
     def backward(h, j):
         return pltpu.make_async_remote_copy(
-            src_ref=loc.at[h, j, pl.ds(0, BACK)], dst_ref=rcv.at[h, j, pl.ds(0, BACK)],
+            src_ref=out.at[h, j], dst_ref=rcv.at[h, j],
             send_sem=bs_sem.at[h, j], recv_sem=br_sem.at[h, j],
             device_id=(dp, lax.max(me - 1, 0)), device_id_type=MESH)
 
@@ -132,18 +188,18 @@
 
             @pl.when((me < nctx - 1) & (j < me))
             def _():
-                loc[h, j, 0:BACK, :] = loc[h, j, 0:BACK, :] + rcv[h, j, 0:BACK, :]
+                out[h, j] = pack_terms(loc[h, j] + unpack_terms(rcv[h, j]))
                 backward(h, j).start()
 
     pr = iota((tokens, 128), 0) - length
     cr = iota((tokens, 128), 1)
     put_k = jnp.where((pr == cr) & (cr < SUMM), 1.0, 0.0).astype(BF16)
-    put_v = jnp.where((pr == cr - SUMM) & (pr >= 0) & (pr < SUMM), 1.0, 0.0).astype(BF16)
+    put_v = jnp.where((pr == cr - SLOT) & (pr >= 0) & (pr < SUMM), 1.0, 0.0).astype(BF16)
     key_parts, value_parts = [], []
 
     def finish(h, back_sum):
         cols = slice(h * D, (h + 1) * D)
-        back = rcv[h, me, :, :]
+        back = unpack_terms(rcv[h, me])
         hi = back.astype(BF16)
         rest = back - hi.astype(F32)
         mid = rest.astype(BF16)
@@ -192,13 +248,12 @@
         dv = dot(p_ref[...], c)
         for j in range(nctx - 1):
             at = j * SLOT
-            tail = pltpu.roll(dv[at:at + SLOT], 2, 0)
-            loc[h, j, 0:48, :] = dk[at:at + 48]
-            loc[h, j, 48:56, :] = dk[at + 48:at + 56] + tail[0:8]
-            loc[h, j, 56:BACK, :] = tail[8:56]
+            loc[h, j, 0:SLOT, :] = dk[at:at + SLOT]
+            loc[h, j, SLOT:2 * SLOT, :] = dv[at:at + SLOT]
 
             @pl.when(me == nctx - 1)
             def _():
+                out[h, j] = pack_terms(loc[h, j])
                 backward(h, j).start()
         key_parts.append(dk[nmem:])
         value_parts.append(dv[nmem:])
@@ -263,32 +318,34 @@
         scatter(k).wait_recv()
         up_sum = up_sum + rs[k]
     blocks = chunk // 128
-    for b in range(blocks):
-        zbuf[me, b * rank:(b + 1) * rank, :] = down[:, b * 128:(b + 1) * 128]
-    zbuf[me, blocks * rank:blocks * rank + ups_each * 8, :] = up_sum
+    first = blocks * rank
+    rows = first + ups_each * 8
+    sums = jnp.concatenate([down[:, b * 128:(b + 1) * 128] for b in range(blocks)] + [up_sum], 0)
+    zbuf[me] = pack_sums(sums, first)
     for k in range(1, nctx):
         spread(k).start()
     for k in range(1, nctx):
         spread_in(k).wait_recv()
-    total = zbuf[0]
+    total = unpack_sums(zbuf[0], first, rows)
     for j in range(1, nctx):
-        total = total + zbuf[j]
-    gat[dp] = total * (ADAPTER_SCALE / (ndp * nctx))
+        total = total + unpack_sums(zbuf[j], first, rows)
+    gat[dp] = pack_sums(total * (ADAPTER_SCALE / (ndp * nctx)), first)
     for k in range(1, ndp):
         gather(k).start()
     for d in range(ndp):
         if d < ndp - 1:
             gather_in(d + 1).wait_recv()
     for d in range(ndp):
+        whole = unpack_sums(gat[d], first, rows)
         for b in range(blocks):
             at = d * chunk + b * 128
-            down_ref[:, at:at + 128] = gat[d, b * rank:(b + 1) * rank, :]
+            down_ref[:, at:at + 128] = whole[b * rank:(b + 1) * rank]
         for u in range(ups_each):
             n = d * ups_each + u
             if n < rank // 8 * kv:
                 at = blocks * rank + u * 8
                 a, b = n // kv * 8, n % kv * 128
-                upg_ref[a:a + 8, b:b + 128] = gat[d, at:at + 8, :]
+                upg_ref[a:a + 8, b:b + 128] = whole[at:at + 8]
 
     stores[3].start()
     stores[4].start()
@@ -336,7 +393,7 @@
     D = HEAD_SIZE
     ups_each = -(-(rank // 8 * kv) // ndp)
     chunk = model // ndp
-    rows = chunk // 128 * rank + ups_each * 8
+    rows = -(-(chunk // 128 * rank + ups_each * 8 + 8) // 16) * 16
     nkeys = nctx * SLOT + tokens
     lanes = groups * tokens
     hbm = pl.BlockSpec(memory_space=pl.ANY)
@@ -370,8 +427,9 @@
             pltpu.VMEM((ndp, rank, tokens), BF16),
             pltpu.VMEM((kv, 2 * SLOT, D), BF16),
             pltpu.VMEM((kv, nctx, 2 * SLOT, D), BF16),
-            pltpu.VMEM((kv, nctx, 128, D), F32),
-            pltpu.VMEM((kv, nctx, 128, D), F32),
+            pltpu.VMEM((kv, nctx, 2 * SLOT, D), F32),
+            pltpu.VMEM((kv, nctx, BACK, D), jnp.int16),
+            pltpu.VMEM((kv, nctx, BACK, D), jnp.int16),
             pltpu.VMEM((nkeys, tokens), F32),
             pltpu.VMEM((nkeys, lanes), F32),
             pltpu.VMEM((nkeys, lanes), F32),
@@ -379,8 +437,8 @@
             pltpu.VMEM((nkeys, lanes), BF16),
             pltpu.VMEM((ndp, ups_each * 8, 128), F32),
             pltpu.VMEM((ndp, ups_each * 8, 128), F32),
-            pltpu.VMEM((nctx, rows, 128), F32),
-            pltpu.VMEM((ndp, rows, 128), F32),
+            pltpu.VMEM((nctx, rows, 128), jnp.int16),
+            pltpu.VMEM((ndp, rows, 128), jnp.int16),
             dma((7,)), dma((5,)),
             dma((kv, nctx)), dma((kv, nctx)),
             dma((kv, nctx)), dma((kv, nctx)),

time: 49.2 us -> 44 us (0.89)
  Pallas kernels: 47.8 us -> 42.6 us
    pallas_call x1, Pallas kernels: 45.7 us -> 40.5 us  [per_device(): pl.pallas_call(functools.partial(kernel, ndp, nctx, kv, groups, tokens, u...]
where the time goes in v3:
time: 44 us; the launch traced here: 43.9 us
  Pallas kernels  42.6 us (97%)
  between operations  1.29 us (3%)
    pallas_call x1, Pallas kernels, per_device(): pl.pallas_call(functools.partial(kernel, ndp, nctx, kv, groups, tokens, u...  40.5 us
    pallas_call x1, Pallas kernels, per_device(): pl.pallas_call(write_out, out_shape=tuple((jax.ShapeDtypeStruct(a.shape,...  2.09 us

profile of v3, /device:TPU:25, one launch (start us, length us, event | category | flops | bytes accessed | tf_op | source)
XLA Modules:
  0.0 43.9 jit_solution(4720355237710323684)
XLA Ops:
  1.3 40.5 %shard_map.119 = (bf16[128,2048]{1,0:T(8,128)(2,1)}, bf16[128,512]{1,0:T(8,128)(2,1)}, bf16[128,512]{1,0:T(8,128)(2,1)}, f32[16,4096]{1,0:T(8,128)}, f32[16,512]{1,0:T(8,128)}) custom-call(s32[1,1]{1,0:T(1,128)S(6)} %copy.13.len_ref, bf16[128,512]{1,0:T(8,128)(2,1)} %bitcast.13, bf16[128,512]{1,0:T(8,128)(2,1)} %bitcast.14, bf16[16,4096]{1,0:T(8,128)(2,1)} %bitcast.15, ...), custom_call_target="tpu_custom_call" | custom-call | tf_op jit(solution)/shard_map/pallas_call | solution.py:402
  41.8 2.1 %shard_map.120 = (bf16[128,2048]{1,0:T(8,128)(2,1)}, bf16[128,512]{1,0:T(8,128)(2,1)}, bf16[128,512]{1,0:T(8,128)(2,1)}, f32[16,4096]{1,0:T(8,128)}, f32[16,512]{1,0:T(8,128)}) custom-call(bf16[128,2048]{1,0:T(8,128)(2,1)} %get-tuple-element.15.refs_0_, bf16[128,512]{1,0:T(8,128)(2,1)} %get-tuple-element.16.refs_1_, ...), custom_call_target="tpu_custom_call" | custom-call | tf_op jit(solution)/shard_map/pallas_call | solution.py:454

commit v4 on v3

--- a/solution.py
+++ b/solution.py
@@ -11,6 +11,7 @@
 HEAD_SIZE = 128
 SUMM = 50
 SLOT = 64
+SENT = 112
 BACK = 112
 STEPS = 64.0
 TOP = 32000.0
@@ -123,13 +124,13 @@
     loads[1].wait()
     length = len_ref[0, 0]
     live = length + SUMM
-    r = iota((SLOT, tokens), 0)
-    pick = jnp.where((iota((SLOT, tokens), 1) == length + r) & (r < SUMM), 1.0, 0.0).astype(BF16)
-    own_k = dot(pick, k_ref[...]).astype(BF16)
-    own_v = dot(pick, v_ref[...]).astype(BF16)
+    r = iota((SENT, tokens), 0)
+    at = iota((SENT, tokens), 1) - length
+    pick_k = jnp.where((at == r) & (r < SUMM), 1.0, 0.0).astype(BF16)
+    pick_v = jnp.where((at == r - SUMM) & (at >= 0) & (at < SUMM), 1.0, 0.0).astype(BF16)
+    sent = (dot(pick_k, k_ref[...]) + dot(pick_v, v_ref[...])).astype(BF16)
     for h in range(kv):
-        own[h, 0:SLOT, :] = own_k[:, h * D:(h + 1) * D]
-        own[h, SLOT:2 * SLOT, :] = own_v[:, h * D:(h + 1) * D]
+        own[h, :, :] = sent[:, h * D:(h + 1) * D]
 
     i = iota((nmem, tokens), 0)
     mask_ref[0:nmem, :] = jnp.where(((i >> 6) < me) & ((i & 63) < SUMM), 1.0, 0.0)
@@ -166,11 +167,8 @@
     for k in range(1, ndp):
         exchange(k).start()
 
-    loads[3].wait()
-    low = dot(hid_ref[...], wt_ref[...], 1, 1).astype(BF16)
     loads[4].wait()
     loads[5].wait()
-    loads[6].wait()
     row = iota((tokens, D), 0)
     cot_mask = jnp.where(row < live, 1.0, 0.0).astype(BF16)
 
@@ -197,7 +195,30 @@
     put_v = jnp.where((pr == cr - SLOT) & (pr >= 0) & (pr < SUMM), 1.0, 0.0).astype(BF16)
     key_parts, value_parts = [], []
 
-    def finish(h, back_sum):
+    def head_rows(h):
+        heads = [h * groups + g for g in range(groups)]
+        q = jnp.concatenate([q_ref[:, a * D:(a + 1) * D] for a in heads], 0)
+        c = jnp.concatenate([cot_ref[:, a * D:(a + 1) * D] * cot_mask for a in heads], 0)
+        return q, c
+
+    def own_scores(h):
+        cols = slice(h * D, (h + 1) * D)
+        q, c = head_rows(h)
+        s = dot(k_ref[:, cols], q, 1, 1)
+        dp_ref[h, nmem:, :] = dot(v_ref[:, cols], c, 1, 1)
+        for g in range(groups):
+            lanes = slice(g * tokens, (g + 1) * tokens)
+            s_ref[h, nmem:, lanes] = jnp.exp(s[:, lanes] * scale) * mask_ref[nmem:, :]
+
+    def query_grads(h):
+        cols = slice(h * D, (h + 1) * D)
+        keys = jnp.concatenate([mem[h, j, 0:SLOT, :] for j in range(nctx)] + [k_ref[:, cols]], 0)
+        dq = dot(ds_ref[h], keys, 0, 0) * scale
+        for g in range(groups):
+            a = h * groups + g
+            gq_ref[:, a * D:(a + 1) * D] = dq[g * tokens:(g + 1) * tokens].astype(BF16)
+
+    def finish(h, back_sum, low):
         cols = slice(h * D, (h + 1) * D)
         back = unpack_terms(rcv[h, me])
         hi = back.astype(BF16)
@@ -222,30 +243,31 @@
         at = (n % ups_each) * 8
         pay[n // ups_each, at:at + 8, :] = jnp.zeros((8, 128), F32)
 
+    own_scores(0)
+    own_scores(1)
     for h in range(kv):
         for k in range(1, nctx):
             @pl.when(me >= k)
             def _():
                 forward(h, k).wait_recv()
-        cols = slice(h * D, (h + 1) * D)
-        keys = jnp.concatenate([mem[h, j, 0:SLOT, :] for j in range(nctx)] + [k_ref[:, cols]], 0)
-        vals = jnp.concatenate([mem[h, j, SLOT:2 * SLOT, :] for j in range(nctx)] + [v_ref[:, cols]], 0)
-        heads = [h * groups + g for g in range(groups)]
-        q = jnp.concatenate([q_ref[:, a * D:(a + 1) * D] for a in heads], 0)
-        c = jnp.concatenate([cot_ref[:, a * D:(a + 1) * D] * cot_mask for a in heads], 0)
-        s_ref[...] = dot(keys, q, 1, 1)
-        dp_ref[...] = dot(vals, c, 1, 1)
+        q, c = head_rows(h)
+        keys = jnp.concatenate([mem[h, j, 0:SLOT, :] for j in range(nctx)], 0)
+        vals = jnp.concatenate(
+            [pltpu.roll(mem[h, j, SENT - SLOT:SENT, :].astype(F32), SLOT - 2, 0).astype(BF16)
+             for j in range(nctx)], 0)
+        s_ref[h, 0:nmem, :] = dot(keys, q, 1, 1)
+        dp_ref[h, 0:nmem, :] = dot(vals, c, 1, 1)
         for g in range(groups):
             lanes = slice(g * tokens, (g + 1) * tokens)
-            e = jnp.exp(s_ref[:, lanes] * scale) * mask_ref[...]
+            e = jnp.exp(s_ref[h, 0:nmem, lanes] * scale) * mask_ref[0:nmem, :]
+            e = jnp.concatenate([e, s_ref[h, nmem:, lanes]], 0)
             attend = e * (1.0 / jnp.sum(e, 0, keepdims=True))
-            grad = dp_ref[:, lanes]
+            grad = dp_ref[h, :, lanes]
             dot_row = jnp.sum(attend * grad, 0, keepdims=True)
             p_ref[:, lanes] = attend.astype(BF16)
-            ds_ref[:, lanes] = (attend * (grad - dot_row)).astype(BF16)
-        ds = ds_ref[...]
-        dk = dot(ds, q) * scale
-        dv = dot(p_ref[...], c)
+            ds_ref[h, :, lanes] = (attend * (grad - dot_row)).astype(BF16)
+        dk = dot(ds_ref[h, 0:nmem, :], q) * scale
+        dv = dot(p_ref[0:nmem, :], c)
         for j in range(nctx - 1):
             at = j * SLOT
             loc[h, j, 0:SLOT, :] = dk[at:at + SLOT]
@@ -255,17 +277,20 @@
             def _():
                 out[h, j] = pack_terms(loc[h, j])
                 backward(h, j).start()
-        key_parts.append(dk[nmem:])
-        value_parts.append(dv[nmem:])
-        dq = dot(ds, keys, 0, 0) * scale
-        for g, a in enumerate(heads):
-            gq_ref[:, a * D:(a + 1) * D] = dq[g * tokens:(g + 1) * tokens].astype(BF16)
         if h > 0:
             chain(h - 1)
-            back_sum = finish(h - 1, back_sum)
-    stores[0].start()
+        key_parts.append(dot(ds_ref[h, nmem:, :], q) * scale)
+        value_parts.append(dot(p_ref[nmem:, :], c))
+        if h + 2 < kv:
+            own_scores(h + 2)
+        if h == 0:
+            loads[3].wait()
+            loads[6].wait()
+            low = dot(hid_ref[...], wt_ref[...], 1, 1).astype(BF16)
+        else:
+            back_sum = finish(h - 1, back_sum, low)
     chain(kv - 1)
-    back_sum = finish(kv - 1, back_sum)
+    back_sum = finish(kv - 1, back_sum, low)
 
     bx[0] = back_sum.astype(BF16)
 
@@ -308,6 +333,8 @@
         scatter(k).start()
     stores[1].start()
     stores[2].start()
+    query_grads(0)
+    query_grads(1)
     down = dot(bx[0], hid_ref[:, columns(dp)])
     up_sum = pay[dp]
     for k in range(1, ndp):
@@ -324,6 +351,9 @@
     zbuf[me] = pack_sums(sums, first)
     for k in range(1, nctx):
         spread(k).start()
+    for h in range(2, kv):
+        query_grads(h)
+    stores[0].start()
     for k in range(1, nctx):
         spread_in(k).wait_recv()
     total = unpack_sums(zbuf[0], first, rows)
@@ -425,16 +455,16 @@
             pltpu.VMEM(hid.shape, BF16),
             pltpu.VMEM((ndp, tokens, chunk), BF16),
             pltpu.VMEM((ndp, rank, tokens), BF16),
-            pltpu.VMEM((kv, 2 * SLOT, D), BF16),
-            pltpu.VMEM((kv, nctx, 2 * SLOT, D), BF16),
+            pltpu.VMEM((kv, SENT, D), BF16),
+            pltpu.VMEM((kv, nctx, SENT, D), BF16),
             pltpu.VMEM((kv, nctx, 2 * SLOT, D), F32),
             pltpu.VMEM((kv, nctx, BACK, D), jnp.int16),
             pltpu.VMEM((kv, nctx, BACK, D), jnp.int16),
             pltpu.VMEM((nkeys, tokens), F32),
-            pltpu.VMEM((nkeys, lanes), F32),
-            pltpu.VMEM((nkeys, lanes), F32),
+            pltpu.VMEM((kv, nkeys, lanes), F32),
+            pltpu.VMEM((kv, nkeys, lanes), F32),
             pltpu.VMEM((nkeys, lanes), BF16),
-            pltpu.VMEM((nkeys, lanes), BF16),
+            pltpu.VMEM((kv, nkeys, lanes), BF16),
             pltpu.VMEM((ndp, ups_each * 8, 128), F32),
             pltpu.VMEM((ndp, ups_each * 8, 128), F32),
             pltpu.VMEM((nctx, rows, 128), jnp.int16),

time: 44 us -> 42.5 us (0.966)
  Pallas kernels: 42.6 us -> 41.1 us
    pallas_call x1, Pallas kernels: 40.5 us -> 39 us  [per_device(): pl.pallas_call(functools.partial(kernel, ndp, nctx, kv, groups, tokens, u...]
where the time goes in v4:
time: 42.5 us; the launch traced here: 42.4 us
  Pallas kernels  41.1 us (97%)
  between operations  1.29 us (3%)
    pallas_call x1, Pallas kernels, per_device(): pl.pallas_call(functools.partial(kernel, ndp, nctx, kv, groups, tokens, u...  39 us
    pallas_call x1, Pallas kernels, per_device(): pl.pallas_call(write_out, out_shape=tuple((jax.ShapeDtypeStruct(a.shape,...  2.09 us

profile of v4, /device:TPU:25, one launch (start us, length us, event | category | flops | bytes accessed | tf_op | source)
XLA Modules:
  0.0 42.4 jit_solution(1866986657815345544)
XLA Ops:
  1.3 39.0 %shard_map.119 = (bf16[128,2048]{1,0:T(8,128)(2,1)}, bf16[128,512]{1,0:T(8,128)(2,1)}, bf16[128,512]{1,0:T(8,128)(2,1)}, f32[16,4096]{1,0:T(8,128)}, f32[16,512]{1,0:T(8,128)}) custom-call(s32[1,1]{1,0:T(1,128)S(6)} %copy.13.len_ref, bf16[128,512]{1,0:T(8,128)(2,1)} %bitcast.13, bf16[128,512]{1,0:T(8,128)(2,1)} %bitcast.14, bf16[16,4096]{1,0:T(8,128)(2,1)} %bitcast.15, ...), custom_call_target="tpu_custom_call" | custom-call | tf_op jit(solution)/shard_map/pallas_call | solution.py:432
  40.3 2.1 %shard_map.120 = (bf16[128,2048]{1,0:T(8,128)(2,1)}, bf16[128,512]{1,0:T(8,128)(2,1)}, bf16[128,512]{1,0:T(8,128)(2,1)}, f32[16,4096]{1,0:T(8,128)}, f32[16,512]{1,0:T(8,128)}) custom-call(bf16[128,2048]{1,0:T(8,128)(2,1)} %get-tuple-element.15.refs_0_, bf16[128,512]{1,0:T(8,128)(2,1)} %get-tuple-element.16.refs_1_, ...), custom_call_target="tpu_custom_call" | custom-call | tf_op jit(solution)/shard_map/pallas_call | solution.py:484
